TPU v7x, 256 devices: a whole 4x4x8 slice. The times are simulated.
256 devices in a mesh: grp: 32 (over x_hi, z, core), ep: 8 (over y, x_lo).
Axes of the slice: x: 4 (x_hi: 2, x_lo: 2; x = x_hi * 2 + x_lo), y: 4, z: 8, core: 2. Of those that a mesh axis runs over, the one named last changes fastest.
Arguments:
- kv_pages: bfloat16 [8192, 64, 576], P(('grp', 'ep')), may hold values from -6 to 6
- page_dest: int32 [8, 1024, 1], P('ep'), may hold values from 0 to 31; in each aligned block of 32 rows (0 to 31, 32 to 63, ..., all dimensions but the last counted through in order) at most 2 rows name the same one
- page_req: int32 [8, 1024], P('ep'), may hold values from 0 to 1
- page_fill: int32 [8, 1024], P('ep'), may hold values from 1 to 64
- queries: bfloat16 [512, 128, 576], P(('grp', 'ep')), may hold values from -250 to 250
- new_latent: bfloat16 [512, 576], P(('grp', 'ep')), may hold values from -6 to 6
- moe_in: bfloat16 [256, 7168], P(('grp', 'ep')), may hold values from -6 to 6
- route_ids: int32 [256, 8], P(('grp', 'ep')), may hold values from 0 to 15, all different within a row
- route_w: float32 [256, 8], P(('grp', 'ep')), may hold values from 0.1 to 0.5
- w_gate: bfloat16 [16, 2048, 7168], P('ep', 'grp'), may hold values from -0.0625 to 0.0625
- w_up: bfloat16 [16, 2048, 7168], P('ep', 'grp'), may hold values from -0.0625 to 0.0625
- w_down: bfloat16 [16, 2048, 7168], P('ep', 'grp'), may hold values from -0.125 to 0.125
Outputs:
- attn_latent: bfloat16 [512, 128, 512], P(('grp', 'ep'))
- moe_out: bfloat16 [256, 7168], P(('grp', 'ep'))
Inputs may be any that keep to these rules, and one draw needn't show every extreme that they name: `page_dest`: at most 2 pages of one device go to one decode group index; some device sends exactly 2 to one.
All inputs are finite; a program needn't handle non-finite values.
Results may differ from a plain program's by a relative error of at most 0.006.
Values may be sent and summed in bfloat16 or wider, within the bound.
A program may use at most 128 MiB of HBM per device.

v0:
```python
import jax
import jax.numpy as jnp
from jax import lax
from jax.sharding import PartitionSpec as P

KV_L = 512
EXPERTS = 16


SCALE = 192.0 ** (-0.5)


def page_ranks(dest, n_grp):
    onehot = (dest[:, :, None] == jnp.arange(n_grp, dtype=jnp.int32)[None, None, :]).astype(
        jnp.int32
    )
    before = jnp.cumsum(onehot, axis=1) - onehot
    return jnp.sum(before * onehot, axis=2)


def attend(rows, own_key, keys, slot_req, slot_fill, latent_width):
    count = rows.shape[0]
    flat = keys.reshape(-1, keys.shape[-1])
    scores = jnp.einsum("rhc,kc->rhk", rows, flat, preferred_element_type=jnp.float32) * SCALE
    own_score = jnp.einsum("rhc,rc->rh", rows, own_key, preferred_element_type=jnp.float32) * SCALE
    position = jnp.arange(keys.shape[1], dtype=jnp.int32)
    live = position[None, :] < slot_fill[:, None]
    mine = slot_req[None, :, None] == jnp.arange(count, dtype=jnp.int32)[:, None, None]
    mask = (mine & live[None, :, :]).reshape(count, 1, -1)
    peak = jnp.maximum(jnp.max(jnp.where(mask, scores, -jnp.inf), axis=2), own_score)
    weights = jnp.where(mask, jnp.exp(scores - peak[:, :, None]), 0.0)
    own_weight = jnp.exp(own_score - peak)
    total = jnp.sum(weights, axis=2) + own_weight
    summed = jnp.einsum(
        "rhk,kc->rhc",
        weights.astype(jnp.bfloat16),
        flat[:, :latent_width],
        preferred_element_type=jnp.float32,
    )
    own_b = own_weight.astype(jnp.bfloat16).astype(jnp.float32)
    summed = summed + own_b[:, :, None] * own_key[:, None, :latent_width].astype(jnp.float32)
    return (summed / total[:, :, None]).astype(jnp.bfloat16)


def per_device(
    kv_pages,
    page_dest,
    page_req,
    page_fill,
    queries,
    new_latent,
    moe_in,
    route_ids,
    route_w,
    w_gate,
    w_up,
    w_down,
):
    n_grp = lax.axis_size("grp")
    target = lax.axis_index("grp")
    column = lax.axis_index("ep")
    pages_dev = kv_pages.shape[0]
    page = kv_pages.shape[1]
    width = kv_pages.shape[2]
    cap = max(2, (pages_dev + n_grp - 1) // n_grp)
    dest = page_dest[0, :, 0].reshape(n_grp, pages_dev)
    ranks = page_ranks(dest, n_grp)
    my_dest = lax.dynamic_index_in_dim(dest, target, 0, False)
    my_rank = lax.dynamic_index_in_dim(ranks, target, 0, False)
    groups = jnp.arange(n_grp, dtype=jnp.int32)
    slots = jnp.arange(cap, dtype=jnp.int32)
    outward = (my_dest[None, None, :] == groups[:, None, None]) & (
        my_rank[None, None, :] == slots[None, :, None]
    )
    outward = outward.astype(jnp.int32)
    pick = jnp.sum(outward * jnp.arange(pages_dev, dtype=jnp.int32)[None, None, :], axis=2)
    used = jnp.sum(outward, axis=2)
    outgoing = jnp.take(kv_pages, pick.reshape(-1), axis=0).reshape(n_grp, cap, page, width)
    outgoing = outgoing * used[:, :, None, None].astype(jnp.bfloat16)
    arrived = lax.all_to_all(outgoing, "grp", split_axis=0, concat_axis=0, tiled=True)
    inward = ((dest == target)[:, :, None] & (ranks[:, :, None] == slots[None, None, :])).astype(
        jnp.int32
    )
    req_tab = page_req[0].reshape(n_grp, pages_dev)
    fill_tab = page_fill[0].reshape(n_grp, pages_dev)
    slot_req = jnp.sum(inward * req_tab[:, :, None], axis=1).reshape(-1)
    slot_fill = jnp.sum(inward * fill_tab[:, :, None], axis=1).reshape(-1)
    chosen = (route_ids[:, :, None] == jnp.arange(EXPERTS, dtype=jnp.int32)[None, None, :]).astype(
        jnp.float32
    )
    gates = jnp.sum(chosen * route_w[:, :, None], axis=1).astype(jnp.bfloat16)
    tokens_all, gates_all = (
        lax.all_gather(moe_in, ("grp", "ep"), axis=0, tiled=True),
        lax.all_gather(gates, ("grp", "ep"), axis=0, tiled=True),
    )
    attn_latent = attend(
        queries, new_latent, arrived.reshape(-1, page, width), slot_req, slot_fill, KV_L
    )
    exp_dev = w_gate.shape[0]
    local_gates = lax.dynamic_slice_in_dim(gates_all, column * exp_dev, exp_dev, 1).astype(
        jnp.float32
    )
    first = jnp.einsum("td,efd->tef", tokens_all, w_gate, preferred_element_type=jnp.float32)
    second = jnp.einsum("td,efd->tef", tokens_all, w_up, preferred_element_type=jnp.float32)
    hidden = (jax.nn.silu(first) * second).astype(jnp.bfloat16)
    tok_dev = moe_in.shape[0]
    summed = jnp.zeros((tok_dev * lax.axis_size(("grp", "ep")), w_down.shape[2]), jnp.float32)
    for expert in range(exp_dev):
        summed = summed + local_gates[:, expert : expert + 1] * jnp.dot(
            hidden[:, expert], w_down[expert], preferred_element_type=jnp.float32
        )
    mixed = lax.psum_scatter(summed, ("grp", "ep"), scatter_dimension=0, tiled=True)
    return (attn_latent, mixed.astype(jnp.bfloat16))


def solution(mesh):
    return jax.shard_map(
        per_device,
        mesh=mesh,
        in_specs=(
            P(("grp", "ep"), None, None),
            P("ep", None, None),
            P("ep", None),
            P("ep", None),
            P(("grp", "ep"), None, None),
            P(("grp", "ep"), None),
            P(("grp", "ep"), None),
            P(("grp", "ep"), None),
            P(("grp", "ep"), None),
            P("ep", "grp", None),
            P("ep", "grp", None),
            P("ep", "grp", None),
        ),
        out_specs=(P(("grp", "ep"), None, None), P(("grp", "ep"), None)),
        check_vma=False,
    )
```

profile of v0, /device:TPU:1, one launch (start us, length us, event | category | flops | bytes accessed | tf_op | source)
XLA Modules:
  0.0 952.1 jit_solution(16804812268294638718)
XLA Ops:
  7.2 0.7 all-gather.4.cloned.1.call-update
  7.9 0.5 broadcast.203
  8.4 1.3 reduce.20
  9.9 1.0 fusion.46
  11.0 0.2 dynamic-slice_reduce_fusion
  11.8 3.5 gather_fusion
  15.3 5.6 select_multiply_fusion
  20.9 12.8 %all-to-all-start = ((bf16[32,2,64,576]{3,2,1,0:T(8,128)(2,1)}), bf16[32,2,64,576]{3,2,1,0:T(8,128)(2,1)}, u32[]{:S(2)}, u32[]{:S(2)}) async-start(bf16[32,2,64,576]{3,2,1,0:T(8,128)(2,1)} %select_multiply_fusion), calls=%async_computation | async-start | bytes 10485760 | tf_op jit(solution)/shard_map/all_to_all | solution.py:80
  33.8 0.7 reduce.21
  34.5 0.7 reduce.22
  36.4 0.2 dynamic-update-slice
  36.8 162.6 %all-reduce.1 = bf16[256,16]{1,0:T(8,128)(2,1)S(1)} all-reduce(bf16[256,16]{1,0:T(8,128)(2,1)S(1)} %reshape.265), channel_id=2, replica_groups=mesh['grp'=32,'ep'=8] {'grp','ep'}, use_global_device_ids=true, to_apply=%add | all-reduce | flops 4096 | bytes 16384
  199.5 0.2 slice_reduce_fusion
  199.9 568.6 %all-gather.4.cloned.1.call-done = bf16[256,1,7168]{2,1,0:T(2,128)(2,1)} async-done(((bf16[1,1,7168]{2,1,0:T(2,128)(2,1)}), bf16[256,1,7168]{2,1,0:T(2,128)(2,1)}) %all-gather.4.cloned.1.call-update) | async-done | bytes 3670032 | tf_op jit(solution)/shard_map/all_gather | solution.py:93
  768.5 5.2 fusion.5
  773.7 0.5 copy-done.6
  774.2 3.1 fusion.21
  777.3 1.1 convolution_multiply_fusion.1
  778.5 4.1 fusion
  782.6 144.2 %all-reduce.4 = bf16[256,7168]{1,0:T(8,128)(2,1)} all-reduce(f32[256,7168]{1,0:T(8,128)} %fusion), channel_id=3, replica_groups=mesh['grp'=32,'ep'=8] {'grp','ep'}, use_global_device_ids=true, to_apply=%region_9.10.clone | all-reduce | flops 1835008 | bytes 11010048
  926.8 1.5 dynamic-slice_convert_fusion.1
  928.3 5.5 select_reduce_fusion
  933.9 3.2 fusion.7
  937.1 8.1 fusion.27
  (59 shorter events, 2.6 us)
Async XLA Ops:
  7.2 4.6 copy-start
  7.2 761.3 %all-gather.4.cloned.1.call-start = ((), (), s32[]{:S(2)}) async-start(), calls=%async_computation.1 | async-start | bytes 7368704 | tf_op jit(solution)/shard_map/all_gather | solution.py:93
  20.9 12.9 %copy-start.4 = (s32[1,1024]{1,0:T(1,128)S(1)}, s32[1,1024]{1,0:T(1,128)}, u32[]{:S(2)}) copy-start(s32[1,1024]{1,0:T(1,128)} %param.14) | copy-start | bytes 12292
  20.9 13.6 %copy-start.5 = (s32[1,1024]{1,0:T(1,128)S(1)}, s32[1,1024]{1,0:T(1,128)}, u32[]{:S(2)}) copy-start(s32[1,1024]{1,0:T(1,128)} %param.15) | copy-start | bytes 12292
  20.9 15.5 %copy-start.7 = (f32[1,8]{1,0:T(1,128)S(1)}, f32[1,8]{1,0:T(1,128)}, u32[]{:S(2)}) copy-start(f32[1,8]{1,0:T(1,128)} %param.20) | copy-start | bytes 100
  20.9 15.5 %copy-start.8 = (s32[1,8]{1,0:T(1,128)S(1)}, s32[1,8]{1,0:T(1,128)}, u32[]{:S(2)}) copy-start(s32[1,8]{1,0:T(1,128)} %param.19) | copy-start | bytes 100
  20.9 178.8 %copy-start.3 = (bf16[2,576]{1,0:T(2,128)(2,1)S(1)}, bf16[2,576]{1,0:T(2,128)(2,1)}, u32[]{:S(2)}) copy-start(bf16[2,576]{1,0:T(2,128)(2,1)} %param.17) | copy-start | bytes 6916
  20.9 178.8 %copy-start.2 = (bf16[2,128,576]{1,2,0:T(8,128)(2,1)S(1)}, bf16[2,128,576]{1,2,0:T(8,128)(2,1)}, u32[]{:S(2)}) copy-start(bf16[2,128,576]{1,2,0:T(8,128)(2,1)} %param.16) | copy-start | bytes 884740
  20.9 907.4 %all-to-all-start = ((bf16[32,2,64,576]{3,2,1,0:T(8,128)(2,1)}), bf16[32,2,64,576]{3,2,1,0:T(8,128)(2,1)}, u32[]{:S(2)}, u32[]{:S(2)}) async-start(bf16[32,2,64,576]{3,2,1,0:T(8,128)(2,1)} %select_multiply_fusion), calls=%async_computation | async-start | bytes 10485760 | tf_op jit(solution)/shard_map/all_to_all | solution.py:80
  768.5 5.7 copy-start.6
  774.2 3.1 copy-start.1
Sparse Core Ops, SparseCore 0:
  9.9 758.5 all-gather.3
where the time goes:
time: 953 us; the launch traced here: 952 us
  waiting for transfers between devices  569 us (60%)
  blocking collectives  307 us (32%)
  matrix products  27.4 us (3%)
  between operations  14.3 us (2%)
  other arithmetic  13.1 us (1%)
  starting transfers between devices  12.8 us (1%)
    all_gather x1, waiting for transfers between devices, per_device(): lax.all_gather(moe_in, ('grp', 'ep'), axis=0, tiled=True)  569 us
    unnamed x2, blocking collectives  307 us
  transfers between devices with their start and end apart: 2, of which 1 were waited for; matrix products, arithmetic and copies ran while one was open for 3% of the time, Pallas kernels for 0%

commit v1 on v0

--- a/solution.py
+++ b/solution.py
@@ -1,10 +1,283 @@
+import functools
+
 import jax
 import jax.numpy as jnp
 from jax import lax
+from jax.experimental import pallas as pl
+from jax.experimental.pallas import tpu as pltpu
 from jax.sharding import PartitionSpec as P
 
+MESH = pl.DeviceIdType.MESH
+EXPERTS = 16
+HALF = 3584
+GW = HALF + 128
+BF = jnp.bfloat16
+F32 = jnp.float32
+
+
+def coords():
+    g = lax.axis_index("grp")
+    e = lax.axis_index("ep")
+    return (g // 16) * 2 + e % 2, e // 2, (g // 2) % 8, g % 2
+
+
+def device(x, y, z, c):
+    x, y, z, c = (x + 4) % 4, (y + 4) % 4, (z + 8) % 8, (c + 2) % 2
+    return ((x // 2) * 16 + z * 2 + c, y * 2 + x % 2)
+
+
+def ring_member(x, y, m):
+    m = (m + 16) % 16
+    return device(x, y, m // 2, m % 2)
+
+
+def barrier(partners):
+    sem = pltpu.get_barrier_semaphore()
+    for p in partners:
+        pl.semaphore_signal(sem, 1, device_id=p, device_id_type=MESH)
+    pl.semaphore_wait(sem, len(partners))
+
+
+def dot_t(a, b):
+    return lax.dot_general(a, b, (((1,), (1,)), ((), ())), preferred_element_type=F32)
+
+
+def moe_steps(r):
+    x, y, z, c = coords()
+    m = z * 2 + c
+    mate = device(x, y, z, 1 - c)
+
+    def push(src, dst, ss, rs, dev):
+        cp = pltpu.make_async_remote_copy(src, dst, ss, rs, device_id=dev, device_id_type=MESH)
+        cp.start()
+        return cp
+
+    loads = [
+        pltpu.make_async_copy(r["wg"], r["w1"].at[pl.ds(0, 128)], r["lsem"].at[0]),
+        pltpu.make_async_copy(r["wu"], r["w1"].at[pl.ds(128, 128)], r["lsem"].at[1]),
+        pltpu.make_async_copy(r["wd"], r["w2"], r["lsem"].at[2]),
+    ]
+    tok, ra = r["tok"], r["ra"]
+    cps = []
+    for k in range(1, 16):
+        mm = (m + k) % 16
+        cps.append(push(tok.at[mm % 2], ra.at[m], r["sa"].at[0, k], r["sa"].at[1, k], ring_member(x, y, mm)))
+    for cp in loads:
+        cp.start()
+    ra[m] = tok[c]
+    yield
+    for cp in cps:
+        cp.wait()
+    rows = lax.broadcasted_iota(jnp.int32, (464, 512), 0)
+    cols = lax.broadcasted_iota(jnp.int32, (464, 512), 1)
+    pick = jnp.where(cols == (rows % 16) * 32 + rows // 16, 1.0, 0.0).astype(BF)
+    got = jnp.dot(pick, ra[...].reshape(512, 128), preferred_element_type=F32).astype(BF)
+    xb = r["xb"]
+    mine = y * 4 + x
+    for j in range(29):
+        xb[c, mine, :, j * 128 : (j + 1) * 128] = got[j * 16 : (j + 1) * 16]
+    cps = []
+    for i, k in enumerate((2, 1, 3)):
+        cps.append(push(xb.at[c, mine], xb.at[c, mine], r["sb"].at[0, i], r["sb"].at[1, i], device(x + k, y, z, c)))
+    yield
+    for cp in cps:
+        cp.wait()
+    own = xb.at[c, pl.ds(y * 4, 4)]
+    cps = []
+    for i, k in enumerate((2, 1, 3)):
+        cps.append(push(own, own, r["sc"].at[0, i], r["sc"].at[1, i], device(x, y + k, z, c)))
+    dcps = [push(own, own, r["sd"].at[0, 3], r["sd"].at[1, 3], mate)]
+    yield
+    for i, k in ((1, 1), (2, 3), (0, 2)):
+        cps[i].wait()
+        blk = xb.at[c, pl.ds(((y - k + 4) % 4) * 4, 4)]
+        dcps.append(push(blk, blk, r["sd"].at[0, i], r["sd"].at[1, i], mate))
+        yield
+    for cp in dcps:
+        cp.wait()
+    for cp in loads:
+        cp.wait()
+    w1, w2, acc = r["w1"], r["w2"], r["acc"]
+    acc[...] = jnp.zeros_like(acc)
+    for h in range(2):
+
+        def step(k, carry, h=h):
+            at = pl.multiple_of(k * 512, 512)
+            a = xb[h, :, :, pl.ds(at, 512)].reshape(256, 512)
+            b = w1[:, pl.ds(pl.multiple_of(h * HALF + at, 128), 512)]
+            acc[...] += dot_t(a, b)
+            return carry
+
+        lax.fori_loop(0, 7, step, 0)
+    first, second = acc[:, :128], acc[:, 128:]
+    hidden = ((first / (1.0 + jnp.exp(-first))) * second).astype(BF).astype(F32)
+    gates = xb[0, :, :, HALF : HALF + 128].reshape(256, 128).astype(F32)
+    col = lax.axis_index("ep")
+    lane = lax.broadcasted_iota(jnp.int32, (256, 128), 1)
+    g0 = jnp.sum(jnp.where(lane == col * 2, gates, 0.0), axis=1, keepdims=True)
+    g1 = jnp.sum(jnp.where(lane == col * 2 + 1, gates, 0.0), axis=1, keepdims=True)
+    scaled = hidden * jnp.where(lane < 64, g0, g1)
+    hi = scaled.astype(BF)
+    lo = (scaled - hi.astype(F32)).astype(BF)
+    ybf, yown, rc = r["ybf"], r["yown"], r["rc"]
+    hl = jnp.concatenate([hi, lo], axis=1)
+
+    def second_product(h, store):
+        def step(k, carry):
+            at = pl.multiple_of(k * 512, 512)
+            w = w2[:, pl.ds(pl.multiple_of(h * HALF + at, 128), 512)]
+            out = jnp.dot(hl, jnp.concatenate([w, w], axis=0), preferred_element_type=F32)
+            store(at, out.reshape(16, 16, 512))
+            return carry
+
+        lax.fori_loop(0, 7, step, 0)
+
+    def to_mate(at, v):
+        ybf[:, :, pl.ds(at, 512)] = v.astype(BF)
+
+    def to_own(at, v):
+        yown[:, :, pl.ds(at, 512)] = v
+
+    second_product(1 - c, to_mate)
+    cps = []
+    for k in range(4):
+        blk = pl.ds(((y + k) % 4) * 4, 4)
+        cps.append(push(ybf.at[blk], rc.at[blk], r["se"].at[0, k], r["se"].at[1, k], mate))
+    second_product(c, to_own)
+    yield
+    s2, r2, yacc = r["s2"], r["r2"], r["yacc"]
+    ycps = [None] * 3
+    for k in (2, 1, 3, 0):
+        blk = pl.ds(((y + k) % 4) * 4, 4)
+        cps[k].wait()
+
+        def step(q, carry, k=k, blk=blk):
+            at = pl.multiple_of(q * 512, 512)
+            v = yown[blk, :, pl.ds(at, 512)] + rc[blk, :, pl.ds(at, 512)].astype(F32)
+            if k == 0:
+                yacc[:, :, pl.ds(at, 512)] = v
+            else:
+                s2[k - 1, :, :, pl.ds(at, 512)] = v.astype(BF)
+            return carry
+
+        lax.fori_loop(0, 7, step, 0)
+        if k:
+            ycps[k - 1] = push(s2.at[k - 1], r2.at[k - 1], r["sf"].at[0, k], r["sf"].at[1, k], device(x, y + k, z, c))
+    yield
+    for cp in ycps:
+        cp.wait()
+    s3, r3, zacc = r["s3"], r["r3"], r["zacc"]
+    xcps = [None] * 3
+    for k in (2, 1, 3, 0):
+        b = (x + k) % 4
+        v = yacc[b]
+        for i in range(3):
+            v = v + r2[i, b].astype(F32)
+        if k == 0:
+            zacc[...] = v
+        else:
+            s3[k - 1] = v.astype(BF)
+            xcps[k - 1] = push(s3.at[k - 1], r3.at[k - 1], r["sg"].at[0, k], r["sg"].at[1, k], device(x + k, y, z, c))
+    yield
+    for cp in xcps:
+        cp.wait()
+    v = zacc[...]
+    for i in range(3):
+        v = v + r3[i].astype(F32)
+    vb = v.astype(BF)
+    stack = jnp.concatenate([vb[:, j * 128 : (j + 1) * 128] for j in range(28)], axis=0)
+    rows = lax.broadcasted_iota(jnp.int32, (512, 448), 0)
+    cols = lax.broadcasted_iota(jnp.int32, (512, 448), 1)
+    pick = jnp.where(cols == (rows % 32) * 16 + rows // 32, 1.0, 0.0).astype(BF)
+    t4, r4 = r["t4"], r["r4"]
+    t4[...] = jnp.dot(pick, stack, preferred_element_type=F32).astype(BF).reshape(16, 32, 128)
+    cps = []
+    for k in range(1, 16):
+        mm = (m + k) % 16
+        cps.append(push(t4.at[mm], r4.at[m], r["sh"].at[0, k], r["sh"].at[1, k], ring_member(x, y, mm)))
+    r4[m] = t4[m]
+    yield
+    for cp in cps:
+        cp.wait()
+    for h in range(2):
+        tot = r4[h].astype(F32)
+        for i in range(1, 8):
+            tot = tot + r4[2 * i + h].astype(F32)
+        r["mo"][h] = tot.astype(BF)
+
+
+MOE_SCRATCH = dict(
+    w1=pltpu.VMEM((256, 2 * HALF), BF),
+    w2=pltpu.VMEM((128, 2 * HALF), BF),
+    ra=pltpu.VMEM((16, 32, 128), BF),
+    xb=pltpu.VMEM((2, 16, 16, GW), BF),
+    acc=pltpu.VMEM((256, 256), F32),
+    ybf=pltpu.VMEM((16, 16, HALF), BF),
+    yown=pltpu.VMEM((16, 16, HALF), F32),
+    rc=pltpu.VMEM((16, 16, HALF), BF),
+    s2=pltpu.VMEM((3, 4, 16, HALF), BF),
+    r2=pltpu.VMEM((3, 4, 16, HALF), BF),
+    yacc=pltpu.VMEM((4, 16, HALF), F32),
+    s3=pltpu.VMEM((3, 16, HALF), BF),
+    r3=pltpu.VMEM((3, 16, HALF), BF),
+    zacc=pltpu.VMEM((16, HALF), F32),
+    t4=pltpu.VMEM((16, 32, 128), BF),
+    r4=pltpu.VMEM((16, 32, 128), BF),
+    lsem=pltpu.SemaphoreType.DMA((3,)),
+    sa=pltpu.SemaphoreType.DMA((2, 16)),
+    sb=pltpu.SemaphoreType.DMA((2, 3)),
+    sc=pltpu.SemaphoreType.DMA((2, 3)),
+    sd=pltpu.SemaphoreType.DMA((2, 4)),
+    se=pltpu.SemaphoreType.DMA((2, 4)),
+    sf=pltpu.SemaphoreType.DMA((2, 4)),
+    sg=pltpu.SemaphoreType.DMA((2, 4)),
+    sh=pltpu.SemaphoreType.DMA((2, 16)),
+)
+
+
+def moe_partners():
+    x, y, z, c = coords()
+    m = z * 2 + c
+    out = [ring_member(x, y, m + k) for k in range(1, 16)]
+    out += [device(x + k, y, z, c) for k in (1, 2, 3)]
+    out += [device(x, y + k, z, c) for k in (1, 2, 3)]
+    return out
+
+
+def moe_kernel(tok, wg, wu, wd, mo, *scratch):
+    r = dict(zip(MOE_SCRATCH, scratch), tok=tok, wg=wg, wu=wu, wd=wd, mo=mo)
+    barrier(moe_partners())
+    for _ in moe_steps(r):
+        pass
+
+
+def moe_call(moe_in, route_ids, route_w, w_gate, w_up, w_down):
+    chosen = (route_ids[:, :, None] == jnp.arange(EXPERTS, dtype=jnp.int32)[None, None, :]).astype(F32)
+    gates = jnp.sum(chosen * route_w[:, :, None], axis=1).astype(BF)
+    gate_row = jnp.pad(gates, ((0, 0), (0, 112)))
+    tok = jnp.concatenate(
+        [
+            moe_in.reshape(2, 28, 128),
+            jnp.broadcast_to(gate_row[None], (2, 1, 128)),
+            jnp.zeros((2, 3, 128), BF),
+        ],
+        axis=1,
+    )
+    vm = pl.BlockSpec(memory_space=pltpu.VMEM)
+    hb = pl.BlockSpec(memory_space=pl.ANY)
+    out = pl.pallas_call(
+        moe_kernel,
+        name="experts",
+        out_shape=jax.ShapeDtypeStruct((2, 32, 128), BF),
+        in_specs=[vm, hb, hb, hb],
+        out_specs=vm,
+        scratch_shapes=list(MOE_SCRATCH.values()),
+        compiler_params=pltpu.CompilerParams(collective_id=0, has_side_effects=True, vmem_limit_bytes=56 * 2**20),
+    )(tok, w_gate.reshape(128, -1), w_up.reshape(128, -1), w_down.reshape(128, -1))
+    return out[:, :28].reshape(1, 2 * HALF)
+
+
 KV_L = 512
-EXPERTS = 16
 
 
 SCALE = 192.0 ** (-0.5)
@@ -85,32 +358,11 @@
     fill_tab = page_fill[0].reshape(n_grp, pages_dev)
     slot_req = jnp.sum(inward * req_tab[:, :, None], axis=1).reshape(-1)
     slot_fill = jnp.sum(inward * fill_tab[:, :, None], axis=1).reshape(-1)
-    chosen = (route_ids[:, :, None] == jnp.arange(EXPERTS, dtype=jnp.int32)[None, None, :]).astype(
-        jnp.float32
-    )
-    gates = jnp.sum(chosen * route_w[:, :, None], axis=1).astype(jnp.bfloat16)
-    tokens_all, gates_all = (
-        lax.all_gather(moe_in, ("grp", "ep"), axis=0, tiled=True),
-        lax.all_gather(gates, ("grp", "ep"), axis=0, tiled=True),
-    )
     attn_latent = attend(
         queries, new_latent, arrived.reshape(-1, page, width), slot_req, slot_fill, KV_L
     )
-    exp_dev = w_gate.shape[0]
-    local_gates = lax.dynamic_slice_in_dim(gates_all, column * exp_dev, exp_dev, 1).astype(
-        jnp.float32
-    )
-    first = jnp.einsum("td,efd->tef", tokens_all, w_gate, preferred_element_type=jnp.float32)
-    second = jnp.einsum("td,efd->tef", tokens_all, w_up, preferred_element_type=jnp.float32)
-    hidden = (jax.nn.silu(first) * second).astype(jnp.bfloat16)
-    tok_dev = moe_in.shape[0]
-    summed = jnp.zeros((tok_dev * lax.axis_size(("grp", "ep")), w_down.shape[2]), jnp.float32)
-    for expert in range(exp_dev):
-        summed = summed + local_gates[:, expert : expert + 1] * jnp.dot(
-            hidden[:, expert], w_down[expert], preferred_element_type=jnp.float32
-        )
-    mixed = lax.psum_scatter(summed, ("grp", "ep"), scatter_dimension=0, tiled=True)
-    return (attn_latent, mixed.astype(jnp.bfloat16))
+    moe_out = moe_call(moe_in, route_ids, route_w, w_gate, w_up, w_down)
+    return (attn_latent, moe_out)
 
 
 def solution(mesh):

time: 953 us -> 248 us (0.26)
  waiting for transfers between devices: 569 us -> 0.01 us
  blocking collectives: 307 us -> 0 us
  Pallas kernels: 0 us -> 199 us
  matrix products: 27.4 us -> 13.8 us
  between operations: 14.3 us -> 0.87 us
    all_gather x1 -> x0, waiting for transfers between devices: 569 us -> none  [per_device(): lax.all_gather(moe_in, ('grp', 'ep'), axis=0, tiled=True)]
    unnamed x2 -> x0, blocking collectives: 307 us -> none
    pallas_call x0 -> x1, Pallas kernels: none -> 199 us  [moe_call(): pl.pallas_call(moe_kernel, name='experts', out_shape=jax.ShapeDtypeStruct...]
    dot_general x4 -> x0, matrix products: 13.6 us -> none  [the longest x2 5.25 us: per_device(): jnp.dot(hidden[:, expert], w_down[expert], preferred_element_type=jnp.flo...]
  transfers between devices with their start and end apart: 2 -> 1, of which waited for: 1 -> 0; matrix products, arithmetic and copies ran while one was open for 3% -> 2% of each run, Pallas kernels for 0% -> 80%
where the time goes in v1:
time: 248 us
  Pallas kernels  199 us (80%)
  other arithmetic  14.1 us (6%)
  matrix products  13.8 us (6%)
  starting transfers between devices  12.8 us (5%)
  local copies, waits for them, and re-layouts  7.37 us (3%)
    pallas_call x1, Pallas kernels, moe_call(): pl.pallas_call(moe_kernel, name='experts', out_shape=jax.ShapeDtypeStruct...  199 us
    all_to_all x1, starting transfers between devices, per_device(): lax.all_to_all(outgoing, 'grp', split_axis=0, concat_axis=0, tiled=True)  12.8 us
    dot_general x1, matrix products, attend(): jnp.einsum('rhk,kc->rhc', weights.astype(jnp.bfloat16), flat[:, :latent_w...  8.12 us
    mul x1, other arithmetic, per_device(): outgoing = outgoing * used[:, :, None, None].astype(jnp.bfloat16)  5.59 us
    dot_general x1, matrix products, attend(): jnp.einsum('rhc,kc->rhk', rows, flat, preferred_element_type=jnp.float32)  5.54 us
  transfers between devices with their start and end apart: 1, of which 0 were waited for; matrix products, arithmetic and copies ran while one was open for 2% of the time, Pallas kernels for 80%

profile of v1, /device:TPU:1, one launch (start us, length us, event | category | flops | bytes accessed | tf_op | source)
XLA Modules:
  0.0 247.7 jit_solution(15826898316550270379)
XLA Ops:
  0.6 0.5 broadcast.204
  1.2 1.6 reduce.17
  2.9 1.0 fusion.28
  4.0 0.2 dynamic-slice_reduce_fusion
  4.2 0.2 fusion.21
  4.4 0.1 reshape.274
  4.6 0.1 copy.33
  4.7 0.1 copy.35
  4.8 3.5 %gather_fusion = bf16[64,64,576]{2,1,0:T(8,128)(2,1)} fusion(bf16[32,64,576]{2,1,0:T(8,128)(2,1)S(1)} %copy-done, s32[1024]{0:T(1024)S(1)} %pad_clamp_fusion), kind=kCustom, calls=%fused_computation | custom fusion | bytes 9437440 | tf_op jit(solution)/shard_map/jit(_take)/gather | solution.py:351
  8.3 5.6 %select_multiply_fusion = bf16[32,2,64,576]{3,2,1,0:T(8,128)(2,1)} fusion(bf16[32,2,64,576]{3,2,1,0:T(8,128)(2,1)} %bitcast.37, pred[32,2]{1,0:T(8,128)(4,1)S(1)} %copy.33, bf16[32,2]{1,0:T(8,128)(2,1)S(1)} %copy.35), kind=kLoop, calls=%fused_computation.3 | loop fusion | flops 4718592 | bytes 9437376 | tf_op jit(solution)/shard_map/mul | solution.py:352
  13.9 12.8 %all-to-all-start = ((bf16[32,2,64,576]{3,2,1,0:T(8,128)(2,1)}), bf16[32,2,64,576]{3,2,1,0:T(8,128)(2,1)}, u32[]{:S(2)}, u32[]{:S(2)}) async-start(bf16[32,2,64,576]{3,2,1,0:T(8,128)(2,1)} %select_multiply_fusion), calls=%async_computation | async-start | bytes 10485760 | tf_op jit(solution)/shard_map/all_to_all | solution.py:353
  26.8 0.7 reduce.18
  27.6 0.7 reduce.19
  28.3 0.1 select_reduce_fusion.1
  28.6 0.1 lt.52
  28.7 0.2 broadcast_reduce_fusion
  29.1 0.1 eq.123
  29.7 0.7 maximum_maximum_fusion.tok
  30.4 198.8 %experts.1 = bf16[2,32,128]{2,1,0:T(8,128)(2,1)} custom-call(bf16[2,32,128]{2,1,0:T(8,128)(2,1)} %maximum_maximum_fusion.tok, bf16[128,7168]{1,0:T(8,128)(2,1)} %bitcast.38, bf16[128,7168]{1,0:T(8,128)(2,1)} %bitcast.39, bf16[128,7168]{1,0:T(8,128)(2,1)} %bitcast.40), custom_call_target="tpu_custom_call" | custom-call | tf_op jit(solution)/shard_map/experts/pallas_call | solution.py:268
  229.2 1.3 reshape.279
  230.6 0.2 fusion.23
  230.8 5.5 %select_reduce_fusion = (f32[2,128]{1,0:T(2,128)S(1)}, f32[2,128,4096]{1,2,0:T(8,128)S(1)}) fusion(pred[2,4096]{1,0:T(4,128)(4,1)S(1)} %broadcast_and_fusion, bf16[4096,576,1]{1,0,2:T(8,128)(2,1)} %bitcast.4, bf16[2,128,576]{1,2,0:T(8,128)(2,1)S(1)} %copy-done.1), kind=kOutput, calls=%fused_computation.7 | convolution fusion | flops 1211105024 | bytes 9217024 | tf_op jit(solution)/shard_map/rhc,kc->rhk/dot_general | solution.py:297
  236.3 3.2 %fusion.2 = f32[2,128]{1,0:T(2,128)S(1)} fusion(f32[2,128,4096]{1,2,0:T(8,128)S(1)} %get-tuple-element.9, f32[2,128]{1,0:T(2,128)S(1)} %multiply_maximum_fusion, pred[2,4096]{1,0:T(4,128)(4,1)S(1)} %broadcast_and_fusion), kind=kLoop, calls=%fused_computation.8 | loop fusion | flops 3145472 | bytes 4204544 | tf_op jit(solution)/shard_map/reduce_sum | solution.py:306
  239.6 8.1 %fusion.14 = bf16[2,128,512]{2,1,0:T(8,128)(2,1)} fusion(bf16[4096,576]{1,0:T(8,128)(2,1)} %bitcast.3, f32[2,128,4096]{1,2,0:T(8,128)S(1)} %get-tuple-element.9, f32[2,128]{1,0:T(2,128)S(1)} %multiply_maximum_fusion, pred[2,4096]{1,0:T(4,128)(4,1)S(1)} %broadcast_and_fusion, f32[2,128]{1,0:T(2,128)S(1)} %get-tuple-element.7, ...), kind=kOutput, calls=%fused_computation.15 | convolution fusion | flops 1077411840 | bytes 8666112 | tf_op jit(solution)/shard_map/rhk,kc->rhc/dot_general | solution.py:307
  (51 shorter events, 1.4 us)
Async XLA Ops:
  0.6 4.2 %copy-start = (bf16[32,64,576]{2,1,0:T(8,128)(2,1)S(1)}, bf16[32,64,576]{2,1,0:T(8,128)(2,1)}, u32[]{:S(2)}) copy-start(bf16[32,64,576]{2,1,0:T(8,128)(2,1)} %param.12) | copy-start | bytes 7077892
  13.9 12.9 %copy-start.4 = (s32[1,1024]{1,0:T(1,128)S(1)}, s32[1,1024]{1,0:T(1,128)}, u32[]{:S(2)}) copy-start(s32[1,1024]{1,0:T(1,128)} %param.14) | copy-start | bytes 12292
  13.9 13.7 %copy-start.5 = (s32[1,1024]{1,0:T(1,128)S(1)}, s32[1,1024]{1,0:T(1,128)}, u32[]{:S(2)}) copy-start(s32[1,1024]{1,0:T(1,128)} %param.15) | copy-start | bytes 12292
  13.9 15.5 %copy-start.2 = (bf16[1,7168]{1,0:T(2,128)(2,1)S(1)}, bf16[1,7168]{1,0:T(2,128)(2,1)}, u32[]{:S(2)}) copy-start(bf16[1,7168]{1,0:T(2,128)(2,1)} %param.18) | copy-start | bytes 43012
  13.9 15.7 %copy-start.6 = (f32[1,8]{1,0:T(1,128)S(1)}, f32[1,8]{1,0:T(1,128)}, u32[]{:S(2)}) copy-start(f32[1,8]{1,0:T(1,128)} %param.20) | copy-start | bytes 100
  13.9 15.7 %copy-start.7 = (s32[1,8]{1,0:T(1,128)S(1)}, s32[1,8]{1,0:T(1,128)}, u32[]{:S(2)}) copy-start(s32[1,8]{1,0:T(1,128)} %param.19) | copy-start | bytes 100
  13.9 216.8 %all-to-all-start = ((bf16[32,2,64,576]{3,2,1,0:T(8,128)(2,1)}), bf16[32,2,64,576]{3,2,1,0:T(8,128)(2,1)}, u32[]{:S(2)}, u32[]{:S(2)}) async-start(bf16[32,2,64,576]{3,2,1,0:T(8,128)(2,1)} %select_multiply_fusion), calls=%async_computation | async-start | bytes 10485760 | tf_op jit(solution)/shard_map/all_to_all | solution.py:353
  26.7 203.8 %copy-start.3 = (bf16[2,576]{1,0:T(2,128)(2,1)S(1)}, bf16[2,576]{1,0:T(2,128)(2,1)}, u32[]{:S(2)}) copy-start(bf16[2,576]{1,0:T(2,128)(2,1)} %param.17) | copy-start | bytes 6916
  26.7 203.8 %copy-start.1 = (bf16[2,128,576]{1,2,0:T(8,128)(2,1)S(1)}, bf16[2,128,576]{1,2,0:T(8,128)(2,1)}, u32[]{:S(2)}) copy-start(bf16[2,128,576]{1,2,0:T(8,128)(2,1)} %param.16) | copy-start | bytes 884740

commit v2 on v1

v2 whole, which is shorter than its diff:
```python
import functools

import jax
import jax.numpy as jnp
from jax import lax
from jax.experimental import pallas as pl
from jax.experimental.pallas import tpu as pltpu
from jax.sharding import PartitionSpec as P

MESH = pl.DeviceIdType.MESH
EXPERTS = 16
HALF = 3584
QUART = 1792
SPLIT = ((0, 2688), (2688, 896))
PLACE = (0, 2, 3, 1)
GW = HALF + 128
BF = jnp.bfloat16
F32 = jnp.float32


def coords():
    g = lax.axis_index("grp")
    e = lax.axis_index("ep")
    return (g // 16) * 2 + e % 2, e // 2, (g // 2) % 8, g % 2


def device(x, y, z, c):
    x, y, z, c = (x + 4) % 4, (y + 4) % 4, (z + 8) % 8, (c + 2) % 2
    return ((x // 2) * 16 + z * 2 + c, y * 2 + x % 2)


def ring_member(x, y, m):
    m = (m + 16) % 16
    return device(x, y, m // 2, m % 2)


def greet(partners):
    sem = pltpu.get_barrier_semaphore()
    for p in partners:
        pl.semaphore_signal(sem, 1, device_id=p, device_id_type=MESH)


def dot_t(a, b):
    return lax.dot_general(a, b, (((1,), (1,)), ((), ())), preferred_element_type=F32)


def moe_steps(r):
    x, y, z, c = coords()
    m = z * 2 + c
    mate = device(x, y, z, 1 - c)

    def push(src, dst, ss, rs, dev):
        cp = pltpu.make_async_remote_copy(src, dst, ss, rs, device_id=dev, device_id_type=MESH)
        cp.start()
        return cp

    loads = [
        pltpu.make_async_copy(r["wg"], r["w1"].at[pl.ds(0, 128)], r["lsem"].at[0]),
        pltpu.make_async_copy(r["wu"], r["w1"].at[pl.ds(128, 128)], r["lsem"].at[1]),
        pltpu.make_async_copy(r["wd"], r["w2"], r["lsem"].at[2]),
    ]
    tok, ra = r["tok"], r["ra"]
    cps = []
    for k in range(1, 16):
        mm = (m + k) % 16
        cps.append(push(tok.at[mm % 2], ra.at[m], r["sa"].at[0, k], r["sa"].at[1, k], ring_member(x, y, mm)))
    for cp in loads:
        cp.start()
    ra[m] = tok[c]
    yield
    for cp in cps:
        cp.wait()
    rows = lax.broadcasted_iota(jnp.int32, (464, 512), 0)
    cols = lax.broadcasted_iota(jnp.int32, (464, 512), 1)
    pick = jnp.where(cols == (rows % 16) * 32 + rows // 16, 1.0, 0.0).astype(BF)
    got = jnp.dot(pick, ra[...].reshape(512, 128), preferred_element_type=F32).astype(BF)
    xb = r["xb"]
    mine = y * 4 + x
    for j in range(29):
        xb[c, mine, :, j * 128 : (j + 1) * 128] = got[j * 16 : (j + 1) * 16]
    up, down = device(x, y + 1, z, c), device(x, y - 1, z, c)

    def block(ky, kx):
        return ((y - ky + 4) % 4) * 4 + (x - kx + 4) % 4

    bcp, ccp, dcp = {}, {}, {}

    def to_mate(ky):
        blk = xb.at[c, pl.ds(((y - ky + 4) % 4) * 4, 4)]
        dcp[ky] = push(blk, blk, r["sd"].at[0, ky], r["sd"].at[1, ky], mate)

    def along_y(kx):
        blk = xb.at[c, block(0, kx)]
        ccp[1, kx] = push(blk, blk, r["sc"].at[0, 1, kx], r["sc"].at[1, 1, kx], up)
        ccp[3, kx] = push(blk, blk, r["sc"].at[0, 3, kx], r["sc"].at[1, 3, kx], down)

    blk = xb.at[c, mine]
    for k in (1, 3, 2):
        bcp[k] = push(blk, blk, r["sb"].at[0, k], r["sb"].at[1, k], device(x + k, y, z, c))
    along_y(0)
    yield
    for k in (1, 3):
        bcp[k].wait()
        along_y(k)
    yield
    bcp[2].wait()
    along_y(2)
    to_mate(0)
    yield
    for kx in (0, 1, 3, 2):
        for ky in (1, 3):
            ccp[ky, kx].wait()
            if (ky == 1) == (kx in (0, 2)):
                blk = xb.at[c, block(ky, kx)]
                ccp[2, kx] = push(blk, blk, r["sc"].at[0, 2, kx], r["sc"].at[1, 2, kx], up if ky == 1 else down)
        if kx in (1, 3):
            yield
    to_mate(1)
    to_mate(3)
    yield
    w1, w2, acc = r["w1"], r["w2"], r["acc"]

    def first_products(kys, row):
        n = 64 * len(kys)
        for h in range(2):
            for q in range(2):
                at = q * QUART
                a = jnp.concatenate(
                    [xb[h, pl.ds(((y - ky + 4) % 4) * 4, 4), :, at : at + QUART].reshape(64, QUART) for ky in kys], axis=0
                )
                p = dot_t(a, w1[:, h * HALF + at : h * HALF + at + QUART])
                if h + q == 0:
                    acc[row : row + n] = p
                else:
                    acc[row : row + n] += p

    for ky in (0, 1, 3):
        dcp[ky].wait()
    for cp in loads:
        cp.wait()
    first_products((0, 1, 3), 0)
    yield
    for kx in (0, 1, 3, 2):
        ccp[2, kx].wait()
    to_mate(2)
    yield
    dcp[2].wait()
    first_products((2,), 192)
    first, second = acc[:, :128], acc[:, 128:]
    hidden = ((first / (1.0 + jnp.exp(-first))) * second).astype(BF).astype(F32)
    gates = jnp.concatenate(
        [xb[0, pl.ds(((y - ky + 4) % 4) * 4, 4), :, HALF:].reshape(64, 128) for ky in (0, 1, 3, 2)], axis=0
    ).astype(F32)
    col = lax.axis_index("ep")
    lane = lax.broadcasted_iota(jnp.int32, (256, 128), 1)
    g0 = jnp.sum(jnp.where(lane == col * 2, gates, 0.0), axis=1, keepdims=True)
    g1 = jnp.sum(jnp.where(lane == col * 2 + 1, gates, 0.0), axis=1, keepdims=True)
    scaled = hidden * jnp.where(lane < 64, g0, g1)
    hi = scaled.astype(BF)
    lo = (scaled - hi.astype(F32)).astype(BF)
    ybf, yown, rc = r["ybf"], r["yown"], r["rc"]
    hl = jnp.concatenate([hi, lo], axis=1)

    def second_product(h, store):
        def step(k, carry):
            at = pl.multiple_of(k * 512, 512)
            w = w2[:, pl.ds(pl.multiple_of(h * HALF + at, 128), 512)]
            out = jnp.dot(hl, jnp.concatenate([w, w], axis=0), preferred_element_type=F32)
            store(at, out.reshape(4, 4, 16, 512))
            return carry

        lax.fori_loop(0, 7, step, 0)

    def keep_bf(at, v):
        ybf[:, :, :, pl.ds(at, 512)] = v.astype(BF)

    def to_own(at, v):
        yown[:, :, :, pl.ds(at, 512)] = v

    second_product(1 - c, keep_bf)
    cps = {i: push(ybf.at[i], rc.at[i], r["se"].at[0, i], r["se"].at[1, i], mate) for i in (3, 2, 1, 0)}
    second_product(c, to_own)
    yield
    s2, r2, yacc = [r["s2a"], r["s2b"]], [r["r2a"], r["r2b"]], [r["yacca"], r["yaccb"]]

    def share(p, k, blk):
        def step(q, carry):
            at = pl.multiple_of(q * 896, 128)
            cols = pl.ds(pl.multiple_of(SPLIT[p][0] + at, 128), 896)
            if p == 0:
                v = yown[blk, :, :, cols] + rc[blk, :, :, cols].astype(F32)
            else:
                v = yown[:, blk, :, cols] + rc[:, blk, :, cols].astype(F32)
            if k == 0:
                yacc[p][:, :, pl.ds(at, 896)] = v
            else:
                s2[p][k - 1, :, :, pl.ds(at, 896)] = v.astype(BF)
            return carry

        lax.fori_loop(0, SPLIT[p][1] // 896, step, 0)

    def far_side(p, k):
        return device(x, y + k, z, c) if p == 0 else device(x + k, y, z, c)

    fcps = {}
    for k in (2, 1, 3):
        cps[PLACE[k]].wait()
        share(0, k, PLACE[k])
        fcps[0, k] = push(s2[0].at[k - 1], r2[0].at[k - 1], r["sf"].at[0, 0, k], r["sf"].at[1, 0, k], far_side(0, k))
    cps[0].wait()
    for k in (2, 1, 3):
        share(1, k, (x + k) % 4)
        fcps[1, k] = push(s2[1].at[k - 1], r2[1].at[k - 1], r["sf"].at[0, 1, k], r["sf"].at[1, 1, k], far_side(1, k))
    share(0, 0, 0)
    share(1, 0, x)
    yield
    s3, r3, zacc = [r["s3a"], r["s3b"]], [r["r3a"], r["r3b"]], [r["zacca"], r["zaccb"]]
    gcps = {}
    for p in range(2):
        for k in (1, 3, 2):
            fcps[p, k].wait()
        for k in (2, 1, 3, 0):
            b = PLACE[k] if p else (x + k) % 4
            v = yacc[p][b]
            for i in range(3):
                v = v + r2[p][i, b].astype(F32)
            if k == 0:
                zacc[p][...] = v
            else:
                s3[p][k - 1] = v.astype(BF)
                gcps[p, k] = push(s3[p].at[k - 1], r3[p].at[k - 1], r["sg"].at[0, p, k], r["sg"].at[1, p, k], far_side(1 - p, k))
    yield
    for cp in gcps.values():
        cp.wait()
    parts = []
    for p in range(2):
        v = zacc[p][...]
        for i in range(3):
            v = v + r3[p][i].astype(F32)
        parts.append(v)
    v = jnp.concatenate(parts, axis=1)
    vb = v.astype(BF)
    stack = jnp.concatenate([vb[:, j * 128 : (j + 1) * 128] for j in range(28)], axis=0)
    rows = lax.broadcasted_iota(jnp.int32, (512, 448), 0)
    cols = lax.broadcasted_iota(jnp.int32, (512, 448), 1)
    pick = jnp.where(cols == (rows % 32) * 16 + rows // 32, 1.0, 0.0).astype(BF)
    t4, r4 = r["t4"], r["r4"]
    t4[...] = jnp.dot(pick, stack, preferred_element_type=F32).astype(BF).reshape(16, 32, 128)
    cps = []
    for k in range(1, 16):
        mm = (m + k) % 16
        cps.append(push(t4.at[mm], r4.at[m], r["sh"].at[0, k], r["sh"].at[1, k], ring_member(x, y, mm)))
    r4[m] = t4[m]
    yield
    for cp in cps:
        cp.wait()
    row = []
    for h in range(2):
        tot = r4[h].astype(F32)
        for i in range(1, 8):
            tot = tot + r4[2 * i + h].astype(F32)
        row += [tot[j : j + 1] for j in range(28)]
    r["mo"][...] = jnp.concatenate(row, axis=1).astype(BF)


MOE_SCRATCH = dict(
    w1=pltpu.VMEM((256, 2 * HALF), BF),
    w2=pltpu.VMEM((128, 2 * HALF), BF),
    ra=pltpu.VMEM((16, 32, 128), BF),
    xb=pltpu.VMEM((2, 16, 16, GW), BF),
    acc=pltpu.VMEM((256, 256), F32),
    ybf=pltpu.VMEM((4, 4, 16, HALF), BF),
    yown=pltpu.VMEM((4, 4, 16, HALF), F32),
    rc=pltpu.VMEM((4, 4, 16, HALF), BF),
    s2a=pltpu.VMEM((3, 4, 16, 2688), BF),
    s2b=pltpu.VMEM((3, 4, 16, 896), BF),
    r2a=pltpu.VMEM((3, 4, 16, 2688), BF),
    r2b=pltpu.VMEM((3, 4, 16, 896), BF),
    yacca=pltpu.VMEM((4, 16, 2688), F32),
    yaccb=pltpu.VMEM((4, 16, 896), F32),
    s3a=pltpu.VMEM((3, 16, 2688), BF),
    s3b=pltpu.VMEM((3, 16, 896), BF),
    r3a=pltpu.VMEM((3, 16, 2688), BF),
    r3b=pltpu.VMEM((3, 16, 896), BF),
    zacca=pltpu.VMEM((16, 2688), F32),
    zaccb=pltpu.VMEM((16, 896), F32),
    t4=pltpu.VMEM((16, 32, 128), BF),
    r4=pltpu.VMEM((16, 32, 128), BF),
    lsem=pltpu.SemaphoreType.DMA((3,)),
    sa=pltpu.SemaphoreType.DMA((2, 16)),
    sb=pltpu.SemaphoreType.DMA((2, 4)),
    sc=pltpu.SemaphoreType.DMA((2, 4, 4)),
    sd=pltpu.SemaphoreType.DMA((2, 4)),
    se=pltpu.SemaphoreType.DMA((2, 4)),
    sf=pltpu.SemaphoreType.DMA((2, 2, 4)),
    sg=pltpu.SemaphoreType.DMA((2, 2, 4)),
    sh=pltpu.SemaphoreType.DMA((2, 16)),
)


def moe_partners():
    x, y, z, c = coords()
    m = z * 2 + c
    out = [ring_member(x, y, m + k) for k in range(1, 16)]
    out += [device(x + k, y, z, c) for k in (1, 2, 3)]
    out += [device(x, y + k, z, c) for k in (1, 2, 3)]
    return out


SCALE = 192.0 ** (-0.5)
NEG = -1e30
KV_L = 512
ORDER = (4, 3, -3, 2, -2, 1, -1, 0)


def lane_of(s):
    return s // 2, s % 2


def attn_steps(r):
    x, y, z, c = coords()
    xh, xl = x // 2, x % 2
    own = xh * 2 + c
    right, left = device(x, y, z + 1, c), device(x, y, z - 1, c)
    ahead = (right, left)

    def push(src, dst, sems, at, dev):
        cp = pltpu.make_async_remote_copy(src, dst, sems.at[(0, *at)], sems.at[(1, *at)], device_id=dev, device_id_type=MESH)
        cp.start()
        return cp

    qin, kvv, pick, mask, nl = r["q"], r["kvv"], r["pick"], r["mask"], r["nl"]
    ql, kl, ol = r["ql"], r["kl"], r["ol"]
    r["qcp"].wait()
    for i in range(2):
        ql[0, i * 160 : i * 160 + 128] = qin[i, :KV_L].astype(F32).T.astype(BF)
    rope = jnp.concatenate([qin[0, KV_L:].astype(F32), qin[1, KV_L:].astype(F32)], axis=0).T.astype(BF)
    for i in range(4):
        ql[0, 128:160, i * 128 : (i + 1) * 128] = rope[i * 32 : (i + 1) * 32]
    qcp = {}

    def send_q(d, hop):
        at = 0 if hop == 0 else 1 + d * 3 + hop - 1
        to = 1 + d * 3 + hop
        qcp[d, hop + 1] = push(ql.at[at], ql.at[to], r["sq"], (d, hop), ahead[d])

    def send_q4(d):
        at = 1 + d * 3 + 2
        rows = pl.ds(160, 128) if d else pl.ds(0, 160)
        qcp[d, 4] = push(ql.at[at, rows], ql.at[7, rows], r["sq"], (d, 3), ahead[d])

    xcp, lcp = r["xcp"], r["lcp"]

    def gather(i):
        zt = (z + ORDER[i] + 8) % 8

        def copy_page(n, carry):
            k, t = n // 2, n % 2
            to = ((xh + k // 2) % 2) * 16 + zt * 2 + (c + k) % 2
            page = kvv[pick[t, to]]
            at = pl.multiple_of(t * 32, 32)
            ol[i, k, pl.ds(at, 32)] = page[:32, :KV_L]
            ol[i, k, pl.ds(at + 64, 32)] = page[32:, :KV_L]
            rope = jnp.concatenate([page[:32, KV_L:], page[32:, KV_L:]], axis=1)
            for j in range(2):
                ol[i, k, 128:144, pl.ds(pl.multiple_of((t * 2 + j) * 128, 128), 128)] = rope[j * 16 : (j + 1) * 16]
            return carry

        lax.fori_loop(0, 8, copy_page, 0)

    r["kvcp"].wait()
    for i in range(8):
        gather(i)
    yield
    send_q(0, 0)
    send_q(1, 0)
    yield
    for hop in (1, 2, 3):
        for d in (0, 1):
            qcp[d, hop].wait()
            if hop < 3:
                send_q(d, hop)
            else:
                send_q4(d)
        yield
    lane = lax.broadcasted_iota(jnp.int32, (128, 128), 1)
    pacc, pm, ps = r["pacc"], r["pm"], r["ps"]
    ca, cs, sa, ss = r["ca"], r["cs"], r["cout"], r["csout"]

    def rope_of(at):
        return jnp.concatenate([ql[at, 128:160, j * 128 : (j + 1) * 128] for j in range(4)], axis=0)

    def partial(i, at):
        q = jnp.concatenate([ql[at, :128], ql[at, 160:]], axis=0)
        a = rope_of(at).astype(F32)
        b = pltpu.roll(a, 64, 1)
        lo = jnp.concatenate([jnp.where(lane < 64, a, 0.0), jnp.where(lane < 64, b, 0.0)], axis=0).astype(BF)
        hi = jnp.concatenate([jnp.where(lane >= 64, b, 0.0), jnp.where(lane >= 64, a, 0.0)], axis=0).astype(BF)
        kv = jnp.concatenate(
            [kl[i, n, 128:144, j * 128 : (j + 1) * 128] for n in range(4) for j in range(4)], axis=0
        )
        near, far = kl[i, :, :64].reshape(256, KV_L), kl[i, :, 64:128].reshape(256, KV_L)
        s = jnp.concatenate(
            [
                dot_t(q, near) + dot_t(lo, kv),
                dot_t(q, far) + dot_t(hi, kv),
            ],
            axis=1,
        ) * SCALE
        live = jnp.concatenate(
            [jnp.broadcast_to(mask[h, i : i + 1], (128, 512)) for h in range(2)], axis=0
        ) > 0.5
        peak = jnp.max(jnp.where(live, s, NEG), axis=1, keepdims=True)
        w = jnp.where(live, jnp.exp(s - peak), 0.0)
        pm[...] = jnp.broadcast_to(peak, (256, 128))
        ps[...] = jnp.broadcast_to(jnp.sum(w, axis=1, keepdims=True), (256, 128))
        wb = w.astype(BF)
        pacc[...] = jnp.dot(wb[:, :256], near, preferred_element_type=F32) + jnp.dot(
            wb[:, 256:], far, preferred_element_type=F32
        )

    def mine(i):
        rows = pl.ds(i * 128, 128)
        return pm[rows, 0:1], ps[rows, 0:1], pacc[rows]

    def merge(a, b):
        peak = jnp.maximum(a[0], b[0])
        u, v = jnp.exp(a[0] - peak), jnp.exp(b[0] - peak)
        return peak, a[1] * u + b[1] * v, a[2] * u + b[2] * v

    ccp = {}

    def send_part(d, dist, i, part):
        at = (d * 4 + dist - 1) * 2 + i
        sa[at] = part[2].astype(BF)
        ss[at] = jnp.where(lane == 0, part[0], part[1]).T[:8]
        ccp[d, dist, i] = [
            push(sa.at[at], ca.at[at], r["sch"], (0, at), ahead[d]),
            push(ss.at[at], cs.at[at], r["sch"], (1, at), ahead[d]),
        ]

    def came(d, dist, i):
        for cp in ccp[d, dist, i]:
            cp.wait()
        at = (d * 4 + dist - 1) * 2 + i
        st = jnp.concatenate([cs[at]] * 16, axis=0).T
        return st[:, 0:1], st[:, 1:2], ca[at].astype(F32)

    for i, dz in enumerate(ORDER):
        r["ready"](i)
        for k in (2, 3, 1):
            xcp[i, k].wait_recv()
        lcp[i].wait()
        if dz == 4:
            for d in (0, 1):
                qcp[d, 4].wait()
            partial(i, 7)
            for d in (0, 1):
                send_part(d, 4, d, mine(d))
            yield
            continue
        if dz:
            d = 0 if dz > 0 else 1
            at = 1 + (1 - d) * 3 + abs(dz) - 1
            partial(i, at)
            yield
            for part in (d, 1 - d):
                v = mine(part)
                if abs(dz) < 3 or part == d:
                    v = merge(came(d, abs(dz) + 1, part), v)
                send_part(d, abs(dz), part, v)
            yield
            continue
        partial(i, 0)
        own_rope = jnp.concatenate([nl[0:1, KV_L:], nl[1:2, KV_L:]], axis=1).astype(F32)
        for part in range(2):
            key = nl[part : part + 1].astype(F32)
            qv = ql[0, part * 160 : part * 160 + 128].astype(F32)
            rope = jnp.where(lane // 64 == part, rope_of(0).astype(F32) * own_rope, 0.0)
            score = (jnp.sum(qv * key[:, :KV_L], axis=1, keepdims=True) + jnp.sum(rope, axis=1, keepdims=True)) * SCALE
            m0, s0, a0 = mine(part)
            peak = jnp.maximum(m0, score)
            u, w = jnp.exp(m0 - peak), jnp.exp(score - peak)
            rows = pl.ds(part * 128, 128)
            pacc[rows] = a0 * u + w.astype(BF).astype(F32) * key[:, :KV_L]
            ps[rows] = jnp.broadcast_to(s0 * u + w, (128, 128))
            pm[rows] = jnp.broadcast_to(peak, (128, 128))
        yield
        for part in range(2):
            v = mine(part)
            v = merge(v, came(0, 1, part))
            v = merge(v, came(1, 1, part))
            r["ao"][part] = (v[2] / v[1]).astype(BF)


def page_steps(r):
    x, y, z, c = coords()
    own = (x // 2) * 2 + c
    ol, kl, xcp, lcp = r["ol"], r["kl"], r["xcp"], r["lcp"]

    def push(src, dst, at, dev):
        cp = pltpu.make_async_remote_copy(src, dst, r["sx"].at[(0, *at)], r["sx"].at[(1, *at)], device_id=dev, device_id_type=MESH)
        cp.start()
        return cp

    for i in range(8):
        for k in (2, 3, 1):
            to = device(x + 2 * (k // 2), y, z, c + k % 2)
            xcp[i, k] = push(ol.at[i, k], kl.at[i, own], (i, k), to)
        lcp[i] = pltpu.make_async_copy(ol.at[i, 0], kl.at[i, own], r["sl"].at[i])
        lcp[i].start()
        yield
    for cp in xcp.values():
        cp.wait_send()


ATTN_SCRATCH = dict(
    q=pltpu.VMEM((2, 576, 128), BF),
    kvv=pltpu.VMEM((32, 64, 576), BF),
    ql=pltpu.VMEM((8, 288, 512), BF),
    kl=pltpu.VMEM((8, 4, 144, 512), BF),
    ol=pltpu.VMEM((8, 4, 144, 512), BF),
    pacc=pltpu.VMEM((256, 512), F32),
    pm=pltpu.VMEM((256, 128), F32),
    ps=pltpu.VMEM((256, 128), F32),
    ca=pltpu.VMEM((16, 128, 512), BF),
    cs=pltpu.VMEM((16, 8, 128), F32),
    cout=pltpu.VMEM((16, 128, 512), BF),
    csout=pltpu.VMEM((16, 8, 128), F32),
    skv=pltpu.SemaphoreType.DMA,
    sqin=pltpu.SemaphoreType.DMA,
    sq=pltpu.SemaphoreType.DMA((2, 2, 4)),
    sx=pltpu.SemaphoreType.DMA((2, 8, 4)),
    sl=pltpu.SemaphoreType.DMA((8,)),
    sch=pltpu.SemaphoreType.DMA((2, 2, 16)),
)


def attn_partners():
    x, y, z, c = coords()
    return [
        device(x, y, z + 1, c),
        device(x, y, z - 1, c),
        device(x, y, z, 1 - c),
        device(x + 2, y, z, c),
        device(x + 2, y, z, 1 - c),
    ]


def tables_kernel(dest, req, fill, mi, ids, rw, pick, mask, tok, tf):
    g = lax.axis_index("grp")
    xh, z, c = g // 16, (g // 2) % 8, g % 2
    x = mi[...].astype(F32)
    lane = lax.broadcasted_iota(jnp.int32, (1, 128), 1)
    gates = jnp.zeros((1, 128), F32)
    for k in range(8):
        gates = gates + jnp.where(lane == ids[:, k : k + 1], rw[:, k : k + 1], 0.0)
    for h in range(2):
        for j in range(28):
            tf[h, j : j + 1] = x[:, (h * 28 + j) * 128 : (h * 28 + j + 1) * 128]
        tf[h, 28:29] = gates
        tf[h, 29:32] = jnp.zeros((3, 128), F32)
    tok[...] = tf[...].astype(BF)
    rows = lax.broadcasted_iota(jnp.int32, (128, 128), 0)
    cols = lax.broadcasted_iota(jnp.int32, (128, 128), 1)
    earlier = jnp.where((rows // 32 == cols // 32) & (cols < rows), 1.0, 0.0).astype(BF)
    code, found = [], []
    for xs in range(2):
        at = pl.multiple_of((xs * 4 + z // 2) * 128, 128)
        value = (fill[:, pl.ds(at, 128)] + 128 * req[:, pl.ds(at, 128)]).astype(F32)
        quarter = lane // 32 - (z % 2) * 2
        left = jnp.concatenate(
            [
                jnp.where(quarter == 0, value, 0.0),
                jnp.where(quarter == 1, value, 0.0),
                jnp.where(quarter == c, (lane % 32).astype(F32), 0.0),
                jnp.zeros((13, 128), F32),
            ],
            axis=0,
        ).astype(BF)
        goes = jnp.broadcast_to(dest[:, pl.ds(at, 128)].astype(F32), (128, 128)).T == cols.astype(F32)
        onehot = jnp.where(goes, 1.0, 0.0).astype(BF)
        before = jnp.dot(earlier, onehot, preferred_element_type=F32)
        at_rank = [
            jnp.dot(left, jnp.where(goes & (before == t), 1.0, 0.0).astype(BF), preferred_element_type=F32)
            for t in range(2)
        ]
        for cc in range(2):
            for t in range(2):
                code.append(at_rank[t][cc : cc + 1])
        found.append([v[2:3] for v in at_rank])
    pick[...] = jnp.concatenate(
        [jnp.where(xh == 0, found[0][t], found[1][t]).astype(jnp.int32) for t in range(2)], axis=0
    )
    codes = jnp.concatenate(code + [jnp.zeros((120, 128), F32)], axis=0).astype(BF)
    plane = lax.broadcasted_iota(jnp.int32, (16, 128), 0)
    away = jnp.zeros((16, 128), jnp.int32)
    for i, dz in enumerate(ORDER):
        away = jnp.where(plane == i, dz, away)
    target = xh * 16 + ((z + away + 8) % 8) * 2 + c
    goal = jnp.where(lax.broadcasted_iota(jnp.int32, (16, 128), 1) == target, 1.0, 0.0).astype(BF)
    slot = dot_t(goal, codes).astype(BF)
    key = lax.broadcasted_iota(jnp.int32, (128, 512), 1)
    spread = jnp.where((key // 32) % 8 == lax.broadcasted_iota(jnp.int32, (128, 512), 0), 1.0, 0.0).astype(BF)
    full = jnp.dot(slot, spread, preferred_element_type=F32)[:8]
    key = lax.broadcasted_iota(jnp.int32, (8, 512), 1)
    pos = ((key // 256) * 32 + key % 32).astype(F32)
    second = full >= 128.0
    mask[0] = jnp.where((pos < full) & ~second, 1.0, 0.0)
    mask[1] = jnp.where((pos < full - 128.0) & second, 1.0, 0.0)


SCHEDULE = "mskmkkksmmskkkkmsmmmsmsmsssssmssssmssmmss"


def merged_kernel(schedule, pick, kv, q, mask, nl, tok, wg, wu, wd, ao, mo, *scratch):
    n = len(ATTN_SCRATCH)
    ra = dict(zip(ATTN_SCRATCH, scratch[:n]), pick=pick, mask=mask, nl=nl, ao=ao)
    rm = dict(zip(MOE_SCRATCH, scratch[n:]), tok=tok, wg=wg, wu=wu, wd=wd, mo=mo)
    ra["kvcp"] = pltpu.make_async_copy(kv, ra["kvv"], ra["skv"])
    qcp = pltpu.make_async_copy(q, ra["q"], ra["sqin"])
    ra["qcp"] = qcp
    ra["kvcp"].start()
    qcp.start()
    ra["xcp"], ra["lcp"] = {}, {}
    steps = {"s": attn_steps(ra), "m": moe_steps(rm), "k": page_steps(ra)}

    def ready(i):
        while i not in ra["lcp"]:
            next(steps["k"])

    ra["ready"] = ready
    partners = moe_partners() + attn_partners()[-1:]
    greet(partners)
    next(steps["s"])
    pl.semaphore_wait(pltpu.get_barrier_semaphore(), len(partners))
    for s in schedule:
        next(steps[s], None)
    for s in "smk":
        for _ in steps[s]:
            pass


def merged_call(kv_pages, page_dest, page_req, page_fill, queries, new_latent, moe_in, route_ids, route_w, w_gate, w_up, w_down):
    vm = pl.BlockSpec(memory_space=pltpu.VMEM)
    hb = pl.BlockSpec(memory_space=pl.ANY)
    pick, mask, tok = pl.pallas_call(
        tables_kernel,
        name="tables",
        out_shape=(
            jax.ShapeDtypeStruct((2, 128), jnp.int32),
            jax.ShapeDtypeStruct((2, 8, 512), F32),
            jax.ShapeDtypeStruct((2, 32, 128), BF),
        ),
        in_specs=[vm] * 6,
        out_specs=(vm, vm, vm),
        scratch_shapes=[
            pltpu.VMEM((2, 32, 128), F32),
        ],
    )(jnp.swapaxes(page_dest, 1, 2).reshape(1, -1), page_req, page_fill, moe_in, route_ids, route_w)
    return pl.pallas_call(
        functools.partial(merged_kernel, SCHEDULE),
        name="decode",
        out_shape=(jax.ShapeDtypeStruct((2, 128, KV_L), BF), jax.ShapeDtypeStruct((1, 2 * HALF), BF)),
        in_specs=[pl.BlockSpec(memory_space=pltpu.SMEM), hb, hb, vm, vm, vm, hb, hb, hb],
        out_specs=(vm, vm),
        scratch_shapes=list(ATTN_SCRATCH.values()) + list(MOE_SCRATCH.values()),
        compiler_params=pltpu.CompilerParams(collective_id=0, has_side_effects=True, vmem_limit_bytes=60 * 2**20),
    )(pick, kv_pages, jnp.swapaxes(queries, 1, 2), mask, new_latent, tok, w_gate.reshape(128, -1), w_up.reshape(128, -1), w_down.reshape(128, -1))


def solution(mesh):
    return jax.shard_map(
        merged_call,
        mesh=mesh,
        in_specs=(
            P(("grp", "ep"), None, None),
            P("ep", None, None),
            P("ep", None),
            P("ep", None),
            P(("grp", "ep"), None, None),
            P(("grp", "ep"), None),
            P(("grp", "ep"), None),
            P(("grp", "ep"), None),
            P(("grp", "ep"), None),
            P("ep", "grp", None),
            P("ep", "grp", None),
            P("ep", "grp", None),
        ),
        out_specs=(P(("grp", "ep"), None, None), P(("grp", "ep"), None)),
        check_vma=False,
    )
```

time: 248 us -> 106 us (0.43)
  Pallas kernels: 199 us -> 102 us
  other arithmetic: 14.1 us -> 0 us
  matrix products: 13.8 us -> 0 us
  starting transfers between devices: 12.8 us -> 0 us
  local copies, waits for them, and re-layouts: 7.37 us -> 3.06 us
    pallas_call x1 -> x2, Pallas kernels: 199 us -> 102 us  [the longest x1 100 us: merged_call(): pl.pallas_call(functools.partial(merged_kernel, SCHEDULE), name='decode',...]
    dot_general x3 -> x0, matrix products: 13.8 us -> none  [the longest x1 8.12 us: attend(): jnp.einsum('rhk,kc->rhc', weights.astype(jnp.bfloat16), flat[:, :latent_w...]
    all_to_all x1 -> x0, starting transfers between devices: 12.8 us -> none  [per_device(): lax.all_to_all(outgoing, 'grp', split_axis=0, concat_axis=0, tiled=True)]
    mul x1 -> x0, other arithmetic: 5.59 us -> none  [per_device(): outgoing = outgoing * used[:, :, None, None].astype(jnp.bfloat16)]
    reduce_sum x4 -> x0, other arithmetic: 3.63 us -> none  [the longest x1 3.24 us: attend(): total = jnp.sum(weights, axis=2) + own_weight]
    gather x1 -> x0, local copies, waits for them, and re-layouts: 3.53 us -> none  [per_device(): jnp.take(kv_pages, pick.reshape(-1), axis=0)]
    unnamed x4 -> x0, other arithmetic: 3.04 us -> none
    unnamed x17 -> x2, local copies, waits for them, and re-layouts: 0.56 us -> 3.06 us
  transfers between devices with their start and end apart: 1 -> 0, of which waited for: 0 -> 0; matrix products, arithmetic and copies ran while one was open for 2% -> 0% of each run, Pallas kernels for 80% -> 0%
where the time goes in v2:
time: 106 us
  Pallas kernels  102 us (96%)
  local copies, waits for them, and re-layouts  3.06 us (3%)
    pallas_call x1, Pallas kernels, merged_call(): pl.pallas_call(functools.partial(merged_kernel, SCHEDULE), name='decode',...  100 us
    unnamed x2, local copies, waits for them, and re-layouts  3.06 us
    pallas_call x1, Pallas kernels, merged_call(): pl.pallas_call(tables_kernel, name='tables', out_shape=(jax.ShapeDtypeStr...  2.14 us

profile of v2, /device:TPU:1, one launch (start us, length us, event | category | flops | bytes accessed | tf_op | source)
XLA Modules:
  0.0 106.0 jit_solution(3853494067251864807)
XLA Ops:
  0.6 2.1 %tables.1 = (s32[2,128]{1,0:T(2,128)}, f32[2,8,512]{2,1,0:T(8,128)}, bf16[2,32,128]{2,1,0:T(8,128)(2,1)}) custom-call(s32[1,1024]{1,0:T(1,128)} %bitcast.9, s32[1,1024]{1,0:T(1,128)} %req.1, s32[1,1024]{1,0:T(1,128)} %fill.1, bf16[1,7168]{1,0:T(2,128)(2,1)} %mi.1, s32[1,8]{1,0:T(1,128)} %ids.1, f32[1,8]{1,0:T(1,128)} %rw.1), custom_call_target="tpu_custom_call" | custom-call | tf_op jit(solution)/shard_map/tables/pallas_call | solution.py:647
  2.8 100.2 %decode.1 = (bf16[2,128,512]{2,1,0:T(8,128)(2,1)}, bf16[1,7168]{1,0:T(2,128)(2,1)}) custom-call(s32[2,128]{1,0:T(2,128)} %get-tuple-element.5.pick, bf16[32,64,576]{2,1,0:T(8,128)(2,1)} %kv.1, bf16[2,576,128]{2,1,0:T(8,128)(2,1)} %bitcast.8, f32[2,8,512]{2,1,0:T(8,128)} %get-tuple-element.6.mask, bf16[2,576]{1,0:T(2,128)(2,1)} %nl.1, ...), custom_call_target="tpu_custom_call" | custom-call | tf_op jit(solution)/shard_map/decode/pallas_call | solution.py:661
  102.9 1.7 %copy.16 = bf16[2,128,512]{2,1,0:T(8,128)(2,1)} copy(bf16[2,128,512]{2,1,0:T(8,128)(2,1)} %get-tuple-element.10) | data formatting | bytes 524288
  104.6 1.4 %copy.17 = bf16[1,7168]{1,0:T(2,128)(2,1)} copy(bf16[1,7168]{1,0:T(2,128)(2,1)} %get-tuple-element.11) | data formatting | bytes 28672

commit v3 on v2

--- a/solution.py
+++ b/solution.py
@@ -11,7 +11,7 @@
 EXPERTS = 16
 HALF = 3584
 QUART = 1792
-SPLIT = ((0, 2688), (2688, 896))
+SPLIT = ((0, 3072), (3072, 512))
 PLACE = (0, 2, 3, 1)
 GW = HALF + 128
 BF = jnp.bfloat16
@@ -185,19 +185,19 @@
 
     def share(p, k, blk):
         def step(q, carry):
-            at = pl.multiple_of(q * 896, 128)
-            cols = pl.ds(pl.multiple_of(SPLIT[p][0] + at, 128), 896)
+            at = pl.multiple_of(q * 512, 128)
+            cols = pl.ds(pl.multiple_of(SPLIT[p][0] + at, 128), 512)
             if p == 0:
                 v = yown[blk, :, :, cols] + rc[blk, :, :, cols].astype(F32)
             else:
                 v = yown[:, blk, :, cols] + rc[:, blk, :, cols].astype(F32)
             if k == 0:
-                yacc[p][:, :, pl.ds(at, 896)] = v
+                yacc[p][:, :, pl.ds(at, 512)] = v
             else:
-                s2[p][k - 1, :, :, pl.ds(at, 896)] = v.astype(BF)
+                s2[p][k - 1, :, :, pl.ds(at, 512)] = v.astype(BF)
             return carry
 
-        lax.fori_loop(0, SPLIT[p][1] // 896, step, 0)
+        lax.fori_loop(0, SPLIT[p][1] // 512, step, 0)
 
     def far_side(p, k):
         return device(x, y + k, z, c) if p == 0 else device(x + k, y, z, c)
@@ -272,18 +272,18 @@
     ybf=pltpu.VMEM((4, 4, 16, HALF), BF),
     yown=pltpu.VMEM((4, 4, 16, HALF), F32),
     rc=pltpu.VMEM((4, 4, 16, HALF), BF),
-    s2a=pltpu.VMEM((3, 4, 16, 2688), BF),
-    s2b=pltpu.VMEM((3, 4, 16, 896), BF),
-    r2a=pltpu.VMEM((3, 4, 16, 2688), BF),
-    r2b=pltpu.VMEM((3, 4, 16, 896), BF),
-    yacca=pltpu.VMEM((4, 16, 2688), F32),
-    yaccb=pltpu.VMEM((4, 16, 896), F32),
-    s3a=pltpu.VMEM((3, 16, 2688), BF),
-    s3b=pltpu.VMEM((3, 16, 896), BF),
-    r3a=pltpu.VMEM((3, 16, 2688), BF),
-    r3b=pltpu.VMEM((3, 16, 896), BF),
-    zacca=pltpu.VMEM((16, 2688), F32),
-    zaccb=pltpu.VMEM((16, 896), F32),
+    s2a=pltpu.VMEM((3, 4, 16, 3072), BF),
+    s2b=pltpu.VMEM((3, 4, 16, 512), BF),
+    r2a=pltpu.VMEM((3, 4, 16, 3072), BF),
+    r2b=pltpu.VMEM((3, 4, 16, 512), BF),
+    yacca=pltpu.VMEM((4, 16, 3072), F32),
+    yaccb=pltpu.VMEM((4, 16, 512), F32),
+    s3a=pltpu.VMEM((3, 16, 3072), BF),
+    s3b=pltpu.VMEM((3, 16, 512), BF),
+    r3a=pltpu.VMEM((3, 16, 3072), BF),
+    r3b=pltpu.VMEM((3, 16, 512), BF),
+    zacca=pltpu.VMEM((16, 3072), F32),
+    zaccb=pltpu.VMEM((16, 512), F32),
     t4=pltpu.VMEM((16, 32, 128), BF),
     r4=pltpu.VMEM((16, 32, 128), BF),
     lsem=pltpu.SemaphoreType.DMA((3,)),
@@ -610,7 +610,7 @@
     mask[1] = jnp.where((pos < full - 128.0) & second, 1.0, 0.0)
 
 
-SCHEDULE = "mskmkkksmmskkkkmsmmmsmsmsssssmssssmssmmss"
+SCHEDULE = "mskmkkksmmskkkkmsmmmsmsmssmsssssssmssmmss"
 
 
 def merged_kernel(schedule, pick, kv, q, mask, nl, tok, wg, wu, wd, ao, mo, *scratch):
@@ -639,6 +639,11 @@
     for s in "smk":
         for _ in steps[s]:
             pass
+
+
+def finish_kernel(a, b, ao, bo):
+    ao[...] = a[...]
+    bo[...] = b[...]
 
 
 def merged_call(kv_pages, page_dest, page_req, page_fill, queries, new_latent, moe_in, route_ids, route_w, w_gate, w_up, w_down):
@@ -658,15 +663,23 @@
             pltpu.VMEM((2, 32, 128), F32),
         ],
     )(jnp.swapaxes(page_dest, 1, 2).reshape(1, -1), page_req, page_fill, moe_in, route_ids, route_w)
-    return pl.pallas_call(
+    shapes = (jax.ShapeDtypeStruct((2, 128, KV_L), BF), jax.ShapeDtypeStruct((1, 2 * HALF), BF))
+    outs = pl.pallas_call(
         functools.partial(merged_kernel, SCHEDULE),
         name="decode",
-        out_shape=(jax.ShapeDtypeStruct((2, 128, KV_L), BF), jax.ShapeDtypeStruct((1, 2 * HALF), BF)),
+        out_shape=shapes,
         in_specs=[pl.BlockSpec(memory_space=pltpu.SMEM), hb, hb, vm, vm, vm, hb, hb, hb],
         out_specs=(vm, vm),
         scratch_shapes=list(ATTN_SCRATCH.values()) + list(MOE_SCRATCH.values()),
         compiler_params=pltpu.CompilerParams(collective_id=0, has_side_effects=True, vmem_limit_bytes=60 * 2**20),
     )(pick, kv_pages, jnp.swapaxes(queries, 1, 2), mask, new_latent, tok, w_gate.reshape(128, -1), w_up.reshape(128, -1), w_down.reshape(128, -1))
+    return pl.pallas_call(
+        finish_kernel,
+        name="finish",
+        out_shape=shapes,
+        in_specs=[vm, vm],
+        out_specs=(vm, vm),
+    )(*outs)
 
 
 def solution(mesh):

time: 106 us -> 98.5 us (0.929)
  Pallas kernels: 102 us -> 97.6 us
  local copies, waits for them, and re-layouts: 3.06 us -> 0 us
    pallas_call x1, Pallas kernels: 100 us -> 93.7 us  [merged_call(): pl.pallas_call(functools.partial(merged_kernel, SCHEDULE), name='decode',...]
    unnamed x2 -> x0, local copies, waits for them, and re-layouts: 3.06 us -> none
    pallas_call x0 -> x1, Pallas kernels: none -> 1.68 us  [merged_call(): pl.pallas_call(finish_kernel, name='finish', out_shape=shapes, in_specs=[...]
where the time goes in v3:
time: 98.5 us; the launch traced here: 98.2 us
  Pallas kernels  97.6 us (99%)
    pallas_call x1, Pallas kernels, merged_call(): pl.pallas_call(functools.partial(merged_kernel, SCHEDULE), name='decode',...  93.7 us
    pallas_call x1, Pallas kernels, merged_call(): pl.pallas_call(tables_kernel, name='tables', out_shape=(jax.ShapeDtypeStr...  2.14 us

profile of v3, /device:TPU:1, one launch (start us, length us, event | category | flops | bytes accessed | tf_op | source)
XLA Modules:
  0.0 98.2 jit_solution(2132895366805974125)
XLA Ops:
  0.6 2.1 %tables.1 = (s32[2,128]{1,0:T(2,128)}, f32[2,8,512]{2,1,0:T(8,128)}, bf16[2,32,128]{2,1,0:T(8,128)(2,1)}) custom-call(s32[1,1024]{1,0:T(1,128)} %bitcast.9, s32[1,1024]{1,0:T(1,128)} %req.1, s32[1,1024]{1,0:T(1,128)} %fill.1, bf16[1,7168]{1,0:T(2,128)(2,1)} %mi.1, s32[1,8]{1,0:T(1,128)} %ids.1, f32[1,8]{1,0:T(1,128)} %rw.1), custom_call_target="tpu_custom_call" | custom-call | tf_op jit(solution)/shard_map/tables/pallas_call | solution.py:652
  2.8 93.7 %decode.1 = (bf16[2,128,512]{2,1,0:T(8,128)(2,1)}, bf16[1,7168]{1,0:T(2,128)(2,1)}) custom-call(s32[2,128]{1,0:T(2,128)} %get-tuple-element.7.pick, bf16[32,64,576]{2,1,0:T(8,128)(2,1)} %kv.1, bf16[2,576,128]{2,1,0:T(8,128)(2,1)} %bitcast.8, f32[2,8,512]{2,1,0:T(8,128)} %get-tuple-element.8.mask, bf16[2,576]{1,0:T(2,128)(2,1)} %nl.1, ...), custom_call_target="tpu_custom_call" | custom-call | tf_op jit(solution)/shard_map/decode/pallas_call | solution.py:667
  96.5 1.7 %finish.1 = (bf16[2,128,512]{2,1,0:T(8,128)(2,1)}, bf16[1,7168]{1,0:T(2,128)(2,1)}) custom-call(bf16[2,128,512]{2,1,0:T(8,128)(2,1)} %get-tuple-element.10.a, bf16[1,7168]{1,0:T(2,128)(2,1)} %get-tuple-element.11.b), custom_call_target="tpu_custom_call" | custom-call | tf_op jit(solution)/shard_map/finish/pallas_call | solution.py:676

commit v4 on v3

--- a/solution.py
+++ b/solution.py
@@ -163,19 +163,19 @@
 
     def second_product(h, store):
         def step(k, carry):
-            at = pl.multiple_of(k * 512, 512)
-            w = w2[:, pl.ds(pl.multiple_of(h * HALF + at, 128), 512)]
+            at = pl.multiple_of(k * 896, 128)
+            w = w2[:, pl.ds(pl.multiple_of(h * HALF + at, 128), 896)]
             out = jnp.dot(hl, jnp.concatenate([w, w], axis=0), preferred_element_type=F32)
-            store(at, out.reshape(4, 4, 16, 512))
+            store(at, out.reshape(4, 4, 16, 896))
             return carry
 
-        lax.fori_loop(0, 7, step, 0)
+        lax.fori_loop(0, 4, step, 0)
 
     def keep_bf(at, v):
-        ybf[:, :, :, pl.ds(at, 512)] = v.astype(BF)
+        ybf[:, :, :, pl.ds(at, 896)] = v.astype(BF)
 
     def to_own(at, v):
-        yown[:, :, :, pl.ds(at, 512)] = v
+        yown[:, :, :, pl.ds(at, 896)] = v
 
     second_product(1 - c, keep_bf)
     cps = {i: push(ybf.at[i], rc.at[i], r["se"].at[0, i], r["se"].at[1, i], mate) for i in (3, 2, 1, 0)}

time: 98.5 us -> 97.9 us (level)
  no operation moved by 1% of the time
where the time goes in v4:
time: 97.9 us; the launch traced here: 97.6 us
  Pallas kernels  97 us (99%)
    pallas_call x1, Pallas kernels, merged_call(): pl.pallas_call(functools.partial(merged_kernel, SCHEDULE), name='decode',...  93.2 us
    pallas_call x1, Pallas kernels, merged_call(): pl.pallas_call(tables_kernel, name='tables', out_shape=(jax.ShapeDtypeStr...  2.14 us

profile of v4, /device:TPU:1, one launch (start us, length us, event | category | flops | bytes accessed | tf_op | source)
XLA Modules:
  0.0 97.6 jit_solution(10395496588824730439)
XLA Ops:
  0.6 2.1 %tables.1 = (s32[2,128]{1,0:T(2,128)}, f32[2,8,512]{2,1,0:T(8,128)}, bf16[2,32,128]{2,1,0:T(8,128)(2,1)}) custom-call(s32[1,1024]{1,0:T(1,128)} %bitcast.9, s32[1,1024]{1,0:T(1,128)} %req.1, s32[1,1024]{1,0:T(1,128)} %fill.1, bf16[1,7168]{1,0:T(2,128)(2,1)} %mi.1, s32[1,8]{1,0:T(1,128)} %ids.1, f32[1,8]{1,0:T(1,128)} %rw.1), custom_call_target="tpu_custom_call" | custom-call | tf_op jit(solution)/shard_map/tables/pallas_call | solution.py:652
  2.8 93.2 %decode.1 = (bf16[2,128,512]{2,1,0:T(8,128)(2,1)}, bf16[1,7168]{1,0:T(2,128)(2,1)}) custom-call(s32[2,128]{1,0:T(2,128)} %get-tuple-element.7.pick, bf16[32,64,576]{2,1,0:T(8,128)(2,1)} %kv.1, bf16[2,576,128]{2,1,0:T(8,128)(2,1)} %bitcast.8, f32[2,8,512]{2,1,0:T(8,128)} %get-tuple-element.8.mask, bf16[2,576]{1,0:T(2,128)(2,1)} %nl.1, ...), custom_call_target="tpu_custom_call" | custom-call | tf_op jit(solution)/shard_map/decode/pallas_call | solution.py:667
  95.9 1.7 %finish.1 = (bf16[2,128,512]{2,1,0:T(8,128)(2,1)}, bf16[1,7168]{1,0:T(2,128)(2,1)}) custom-call(bf16[2,128,512]{2,1,0:T(8,128)(2,1)} %get-tuple-element.10.a, bf16[1,7168]{1,0:T(2,128)(2,1)} %get-tuple-element.11.b), custom_call_target="tpu_custom_call" | custom-call | tf_op jit(solution)/shard_map/finish/pallas_call | solution.py:676
